TPU v7x, 256 devices: a whole 4x4x8 slice. The times are simulated.
256 devices in a mesh: replica: 32 (over x, z_lo, core), fsdp: 8 (over y, z_hi).
Axes of the slice: x: 4, y: 4, z: 8 (z_hi: 2, z_lo: 4; z = z_hi * 4 + z_lo), core: 2. Of those that a mesh axis runs over, the one named last changes fastest.
Arguments:
- fp8_codes: int32 [32, 4096, 1024], P('replica', 'fsdp'), may hold values from 32 to 207, as said below
- block_scales: int32 [32, 8, 4096], P('replica', None, 'fsdp'), may hold values from 122 to 127
- outer_params: float32 [4096, 1024], P(('fsdp', 'replica')), may hold values from -6 to 6
- outer_momentum: float32 [4096, 1024], P(('fsdp', 'replica')), may hold values from -4 to 4
- activations: bfloat16 [131072, 4096], P(('replica', 'fsdp')), may hold values from -6 to 6
- norm_gain: bfloat16 [4096], replicated, may hold values from 0.099609375 to 1.8984375
- cotangent: bfloat16 [131072, 1024], P(('replica', 'fsdp')), may hold values from -6 to 6
Outputs:
- projected: bfloat16 [131072, 1024], P(('replica', 'fsdp'))
- input_grad: bfloat16 [131072, 4096], P(('replica', 'fsdp'))
- weight_grad: bfloat16 [32, 4096, 1024], P('replica', 'fsdp')
- params_next: float32 [4096, 1024], P(('fsdp', 'replica'))
- momentum_next: float32 [4096, 1024], P(('fsdp', 'replica'))
Inputs may be any that keep to these rules, and one draw needn't show every extreme that they name: `fp8_codes`: e4m3 codes: c // 128 is the sign, (c % 128) // 8 the exponent field, c % 8 the mantissa field; exponent fields lie between 4 and 9.
All inputs are finite; a program needn't handle non-finite values.
Results may differ from a plain program's by a relative error of at most 0.018.
Values may be sent and summed in bfloat16 or wider, within the bound.
A program may use at most 128 MiB of HBM per device.

v0:
```python
import jax
import jax.numpy as jnp
from jax import lax
from jax.sharding import PartitionSpec as P

outer_rate = 0.7
outer_beta = 0.9
epsilon = 1e-05


def decode(code_block, scale_block):
    negative = code_block // 128
    exponent = code_block % 128 // 8
    mantissa = (code_block % 8).astype(jnp.float32)
    normal_value = (1.0 + mantissa / 8.0) * jnp.exp2((exponent - 7).astype(jnp.float32))
    small_value = mantissa / 8.0 * 0.015625
    magnitude = jnp.where(exponent > 0, normal_value, small_value)
    signed = jnp.where(negative > 0, -magnitude, magnitude)
    factor = jnp.exp2((scale_block - 127).astype(jnp.float32))
    row_count = code_block.shape[0]
    blocks = factor.shape[0]
    shaped = signed.reshape(row_count, blocks, code_block.shape[1] // blocks)
    return (shaped * jnp.transpose(factor)[:, :, None]).reshape(code_block.shape)


def shards(
    fp8_codes, block_scales, outer_params, outer_momentum, activations, norm_gain, cotangent
):
    decoded = decode(fp8_codes[0], block_scales[0])
    replicas = lax.axis_size("replica")
    summed = lax.psum(decoded.astype(jnp.bfloat16), "replica").astype(jnp.float32)
    params_all, momentum_all = (
        lax.all_gather(outer_params, "replica", axis=0, tiled=True),
        lax.all_gather(outer_momentum, "replica", axis=0, tiled=True),
    )
    delta = summed / replicas
    momentum_wide = outer_beta * momentum_all + delta
    params_wide = params_all - outer_rate * (delta + outer_beta * momentum_wide)
    weight_block = params_wide.astype(jnp.bfloat16)
    own_rows = outer_params.shape[0]
    offset = lax.axis_index("replica") * own_rows
    params_next = lax.dynamic_slice_in_dim(params_wide, offset, own_rows, 0)
    momentum_next = lax.dynamic_slice_in_dim(momentum_wide, offset, own_rows, 0)
    width = activations.shape[1]
    factor = width ** (-0.5)
    gain_wide = norm_gain.astype(jnp.float32)
    wide_rows = activations.astype(jnp.float32)
    inverse = lax.rsqrt(jnp.mean(wide_rows * wide_rows, axis=-1, keepdims=True) + epsilon)
    unit = wide_rows * inverse
    normed = (unit * gain_wide).astype(jnp.bfloat16)
    columns = normed
    forward_sum = jnp.dot(
        columns,
        lax.all_gather(weight_block, "fsdp", axis=0, tiled=True),
        preferred_element_type=jnp.float32,
    )
    back_sum = jnp.einsum(
        "tk,dk->td",
        cotangent,
        lax.all_gather(weight_block, "fsdp", axis=0, tiled=True),
        preferred_element_type=jnp.float32,
    )
    projected = (forward_sum * factor).astype(jnp.bfloat16)
    back = back_sum * factor * gain_wide
    input_grad = (inverse * (back - unit * jnp.mean(back * unit, axis=-1, keepdims=True))).astype(
        jnp.bfloat16
    )
    columns = normed
    weight_grad = lax.psum_scatter(
        (
            jnp.einsum("td,tk->dk", columns, cotangent, preferred_element_type=jnp.float32) * factor
        ).astype(jnp.bfloat16),
        "fsdp",
        scatter_dimension=0,
        tiled=True,
    )[None]
    return (projected, input_grad, weight_grad, params_next, momentum_next)


def solution(mesh):
    in_specs = (
        P("replica", "fsdp", None),
        P("replica", None, "fsdp"),
        P(("fsdp", "replica"), None),
        P(("fsdp", "replica"), None),
        P(("replica", "fsdp"), None),
        P(),
        P(("replica", "fsdp"), None),
    )
    out_specs = (
        P(("replica", "fsdp"), None),
        P(("replica", "fsdp"), None),
        P("replica", "fsdp", None),
        P(("fsdp", "replica"), None),
        P(("fsdp", "replica"), None),
    )
    return jax.shard_map(shards, mesh=mesh, in_specs=in_specs, out_specs=out_specs, check_vma=False)
```

profile of v0, /device:TPU:1, one launch (start us, length us, event | category | flops | bytes accessed | tf_op | source)
XLA Modules:
  0.0 789.0 jit_solution(17918511048243130725)
XLA Ops:
  7.2 0.0 copy-start
  7.2 0.0 copy-start.3
  7.2 0.0 all-reduce.2.cloned.1.call-start
  7.2 0.9 exponential_bitcast_fusion
  8.1 0.1 copy.13
  8.2 0.6 mul.108
  8.9 0.0 copy-done.3
  8.9 5.5 fusion.13
  14.3 0.0 all-reduce.2.cloned.1.call-update
  14.4 0.0 all-gather.4.cloned.1.call-start
  14.4 0.7 all-gather.4.cloned.1.call-update
  15.1 0.0 all-gather.6.cloned.1.call-start
  15.2 0.7 all-gather.6.cloned.1.call-update
  15.9 0.0 copy-start.4
  15.9 0.0 all-gather.8.cloned.1.call-start
  15.9 280.7 %all-reduce.2.cloned.1.call-done = bf16[512,1024]{1,0:T(8,128)(2,1)} async-done(((bf16[512,1024]{1,0:T(8,128)(2,1)}), bf16[512,1024]{1,0:T(8,128)(2,1)}) %all-reduce.2.cloned.1.call-update) | async-done | bytes 1048592 | tf_op jit(solution)/shard_map/psum | solution.py:31
  296.6 61.6 %all-gather.4.cloned.1.call-done = f32[512,1024]{1,0:T(8,128)} async-done(((f32[16,1024]{1,0:T(8,128)}), f32[512,1024]{1,0:T(8,128)}) %all-gather.4.cloned.1.call-update) | async-done | bytes 2097168 | tf_op jit(solution)/shard_map/all_gather | solution.py:33
  358.1 61.1 %all-gather.6.cloned.1.call-done = f32[512,1024]{1,0:T(8,128)} async-done(((f32[16,1024]{1,0:T(8,128)}), f32[512,1024]{1,0:T(8,128)}) %all-gather.6.cloned.1.call-update) | async-done | bytes 2097168 | tf_op jit(solution)/shard_map/all_gather | solution.py:34
  419.2 5.0 fusion.21
  424.3 0.0 all-gather.8.cloned.1.call-update
  424.3 0.2 reduce-scatter.2.cloned.1.call-start
  424.5 0.0 copy-done.4
  424.5 6.5 copy.12
  431.0 0.0 copy-start.1
  431.0 3.3 fusion.8
  434.3 0.0 copy-done
  434.3 0.2 copy-done.1
  434.5 6.8 multiply_convert_fusion
  441.2 0.0 reduce-scatter.2.cloned.1.call-update
  441.3 1.5 constant_dynamic-slice_fusion
  442.8 153.1 %all-gather.8.cloned.1.call-done = bf16[4096,1024]{1,0:T(8,128)(2,1)} async-done(((bf16[512,1024]{1,0:T(8,128)(2,1)}), bf16[4096,1024]{1,0:T(8,128)(2,1)}) %all-gather.8.cloned.1.call-update) | async-done | bytes 8388624 | tf_op jit(solution)/shard_map/all_gather | solution.py:54
  595.9 0.0 copy-start.2
  595.9 10.4 %fusion.4 = (f32[512]{0:T(512)S(1)}, f32[4096,512]{1,0:T(8,128)S(1)}) fusion(bf16[512,4096]{0,1:T(8,128)(2,1)} %copy.12, f32[4096]{0:T(1024)S(1)} %broadcast_multiply_fusion, f32[512]{0:T(512)S(1)} %add_rsqrt_fusion, bf16[4096,1024]{1,0:T(8,128)(2,1)} %all-gather.8.cloned.1.call-done, bf16[512,1024]{1,0:T(8,128)(2,1)S(1)} %copy-done), kind=kOutput, calls=%fused_computation.7 | convolution fusion | flops 4305452544 | bytes 22040576 | tf_op jit(solution)/shard_map/tk,dk->td/dot_general | solution.py:57
  606.3 0.0 copy-done.2
  606.3 3.2 fusion.7
  609.5 6.3 copy.14
  615.8 10.3 %multiply_convert_fusion.1 = bf16[512,1024]{1,0:T(8,128)(2,1)} fusion(bf16[4096,1024]{1,0:T(8,128)(2,1)} %all-gather.8.cloned.1.call-done, bf16[512,4096]{0,1:T(8,128)(2,1)} %copy.12, f32[4096]{0:T(1024)S(1)} %convert_element_type.42, f32[512]{0:T(512)S(1)} %add_rsqrt_fusion), kind=kOutput, calls=%fused_computation.32 | convolution fusion | flops 4304404480 | bytes 13649920 | tf_op jit(solution)/shard_map/dot_general | solution.py:52
  626.1 156.4 %reduce-scatter.2.cloned.1.call-done = bf16[512,1024]{1,0:T(8,128)(2,1)} async-done(((bf16[4096,1024]{1,0:T(8,128)(2,1)}), bf16[512,1024]{1,0:T(8,128)(2,1)}) %reduce-scatter.2.cloned.1.call-update) | async-done | bytes 1048592 | tf_op jit(solution)/shard_map/reduce_scatter | solution.py:69
  (4 shorter events, 0.0 us)
Async XLA Ops:
  7.2 427.1 %copy-start = (bf16[512,1024]{1,0:T(8,128)(2,1)S(1)}, bf16[512,1024]{1,0:T(8,128)(2,1)}, u32[]{:S(2)}) copy-start(bf16[512,1024]{1,0:T(8,128)(2,1)} %param.13) | copy-start | bytes 3145732
  7.2 1.7 copy-start.3
  7.2 289.4 %all-reduce.2.cloned.1.call-start = ((), (), s32[]{:S(2)}) async-start(), calls=%async_computation.2 | async-start | bytes 2097152 | tf_op jit(solution)/shard_map/psum | solution.py:31
  14.4 343.8 %all-gather.4.cloned.1.call-start = ((), (), s32[]{:S(2)}) async-start(), calls=%async_computation.1 | async-start | bytes 2162688 | tf_op jit(solution)/shard_map/all_gather | solution.py:33
  15.1 404.1 %all-gather.6.cloned.1.call-start = ((), (), s32[]{:S(2)}) async-start(), calls=%async_computation.3 | async-start | bytes 2162688 | tf_op jit(solution)/shard_map/all_gather | solution.py:34
  15.9 408.7 %copy-start.4 = (bf16[4096]{0:T(1024)(128)(2,1)S(1)}, bf16[4096]{0:T(1024)(128)(2,1)}, u32[]{:S(2)}) copy-start(bf16[4096]{0:T(1024)(128)(2,1)} %param.12) | copy-start | bytes 24580
  15.9 580.0 %all-gather.8.cloned.1.call-start = ((), (), s32[]{:S(2)}) async-start(), calls=%async_computation.4 | async-start | bytes 9437184 | tf_op jit(solution)/shard_map/all_gather | solution.py:54
  424.3 358.2 %reduce-scatter.2.cloned.1.call-start = ((), (), s32[]{:S(2)}) async-start(), calls=%async_computation.5 | async-start | bytes 9437184 | tf_op jit(solution)/shard_map/reduce_scatter | solution.py:69
  431.0 3.4 copy-start.1
  595.9 10.4 %copy-start.2 = (bf16[512,4096]{0,1:T(8,128)(2,1)S(1)}, bf16[512,4096]{0,1:T(8,128)(2,1)}, u32[]{:S(2)}) copy-start(bf16[512,4096]{0,1:T(8,128)(2,1)} %copy.12) | copy-start | bytes 12582916
Sparse Core Ops, SparseCore 0:
  14.5 282.0 all-reduce.1
  298.6 59.5 all-gather.3
  360.2 59.0 all-gather.5
  424.4 171.4 all-gather.7
  601.0 181.4 reduce-scatter.1
where the time goes:
time: 789 us
  waiting for transfers between devices  714 us (90%)
  matrix products  27.4 us (3%)
  other arithmetic  17.9 us (2%)
  local copies, waits for them, and re-layouts  15.2 us (2%)
  between operations  13.9 us (2%)
    psum x1, waiting for transfers between devices, shards(): lax.psum(decoded.astype(jnp.bfloat16), 'replica').astype(jnp.float32)  281 us
    reduce_scatter x1, waiting for transfers between devices, shards(): lax.psum_scatter((jnp.einsum('td,tk->dk', columns, cotangent, preferred_e...  156 us
    all_gather x1, waiting for transfers between devices, shards(): lax.all_gather(weight_block, 'fsdp', axis=0, tiled=True)  153 us
    all_gather x1, waiting for transfers between devices, shards(): lax.all_gather(outer_params, 'replica', axis=0, tiled=True)  61.6 us
    all_gather x1, waiting for transfers between devices, shards(): lax.all_gather(outer_momentum, 'replica', axis=0, tiled=True)  61.1 us
  transfers between devices with their start and end apart: 5, of which 5 were waited for; matrix products, arithmetic and copies ran while one was open for 6% of the time, Pallas kernels for 0%

commit v1 on v0

v1 whole, which is shorter than its diff:
```python
import functools

import jax
import jax.numpy as jnp
from jax import lax
from jax.experimental import pallas as pl
from jax.experimental.pallas import tpu as pltpu
from jax.sharding import PartitionSpec as P

outer_rate = 0.7
outer_beta = 0.9
epsilon = 1e-05
BF = jnp.bfloat16
F32 = jnp.float32
MESH = pl.DeviceIdType.MESH
D = 4096
T = 512
K = 1024
FACTOR = D ** (-0.5)


def device(x, y, z, c):
    return ((x * 4 + lax.rem(z, 4)) * 2 + c, y * 2 + lax.div(z, 4))


def kernel(
    codes, scales, params, moment, act, gain, cot,
    proj_o, ig_o, wg_o, pn_o, mn_o,
    codes_v, act_v, cot_v, nrm, inv_v, dec, g1r, g1s, g2r, g2s, g3r, wfull, acc, back,
    rb, ra, ps, own, pr, zs, zr, wgo, prj, mrow,
    lsem, osem, bsem, asem, psem, zsem, gsem, g2sem, g3sem, ysem, agsem, sbsem,
    bss, ass, pss, zss, gss, g2ss, g3ss, yss, zrs, xs, sbs,
):
    r = lax.axis_index("replica")
    f = lax.axis_index("fsdp")
    x, zl, c = lax.div(r, 8), lax.rem(lax.div(r, 2), 4), lax.rem(r, 2)
    y, zh = lax.div(f, 2), lax.rem(f, 2)
    z = zh * 4 + zl
    other = 1 - c
    swap = y + 1 - 2 * lax.rem(y, 2)
    p1 = c * (3 - y) + other * swap
    p2 = c * swap + other * (3 - y)
    q = lax.rem(y + 2, 4)
    sibling = device(x, y, z, other)
    dev_p1, dev_p2 = device(x, p1, z, c), device(x, p2, z, c)
    dev_z4 = device(x, y, lax.rem(z + 4, 8), c)
    xp = [lax.rem(x + d, 4) for d in (1, 2, 3)]
    zlp = [lax.rem(zl + d, 4) for d in (1, 2, 3)]
    yp = [lax.rem(y + d, 4) for d in (1, 2, 3)]
    zup, zdn = lax.rem(z + 1, 8), lax.rem(z + 7, 8)
    dev_zup, dev_zdn = device(x, y, zup, c), device(x, y, zdn, c)
    dev_x = [device(v, y, z, c) for v in xp]
    dev_zl = [device(x, y, zh * 4 + v, c) for v in zlp]
    dev_y = [device(x, v, z, c) for v in yp]

    started = []

    def send(src, dst, ss, rs, to):
        cp = pltpu.make_async_remote_copy(
            src_ref=src, dst_ref=dst, send_sem=ss, recv_sem=rs, device_id=to, device_id_type=MESH
        )
        cp.start()
        started.append(cp)

    def arrived(dst, rs):
        pltpu.make_async_remote_copy(
            src_ref=dst, dst_ref=dst, send_sem=bss, recv_sem=rs, device_id=sibling, device_id_type=MESH
        ).wait_recv()

    load_codes = pltpu.make_async_copy(codes.at[0], codes_v, lsem.at[0])
    load_act = pltpu.make_async_copy(act, act_v, lsem.at[1])
    load_cot = pltpu.make_async_copy(cot, cot_v, lsem.at[2])
    load_codes.start()
    load_act.start()
    load_cot.start()

    barrier = pltpu.get_barrier_semaphore()
    friends = [sibling, dev_z4, dev_zup, dev_zdn, *dev_x, *dev_zl, *dev_y]
    for to in friends:
        pl.semaphore_signal(barrier, inc=1, device_id=to, device_id_type=MESH)
    pl.semaphore_wait(barrier, len(friends))

    send(cot, rb, bss, bsem, dev_p1)

    factors = jnp.exp2((scales[0] - 127).astype(F32)).astype(BF)
    spread = (
        lax.broadcasted_iota(jnp.int32, (8, K), 1) // 128 == lax.broadcasted_iota(jnp.int32, (8, K), 0)
    ).astype(F32).astype(BF)
    acc[...] = lax.dot_general(factors, spread, (((0,), (0,)), ((), ())), preferred_element_type=F32)
    load_codes.wait()

    def decode_half(which):
        def step(g, _):
            rows = pl.ds(pl.multiple_of(g * 32 + which * 16, 16), 16)
            code = codes_v[rows, :]
            field = (code >> 3) & 15
            low = code & 7
            whole = jnp.where(field > 0, low + 8, low * 2) << field
            value = whole.astype(F32) * (acc[rows, :] * (2.0**-10))
            dec[which, g] = jnp.where(code >= 128, -value, value).astype(BF)
            return 0

        lax.fori_loop(0, 16, step, 0)

    decode_half(other)
    send(dec.at[other], g1r, gss, gsem, sibling)
    decode_half(c)
    arrived(g1r, gsem)

    def sum_one(g, _):
        g1s[g] = (dec[c, g].astype(F32) + g1r[g].astype(F32)).astype(BF)
        return 0

    lax.fori_loop(0, 16, sum_one, 0)
    for i in range(3):
        send(g1s.at[pl.ds(xp[i] * 4, 4)], g2r.at[i], g2ss.at[i], g2sem.at[i], dev_x[i])

    load_act.wait()
    gain_row = gain[...].astype(F32)

    def norm(t, _):
        rows = pl.ds(pl.multiple_of(t * 32, 32), 32)
        total = jnp.zeros((32, 128), F32)
        for j in range(32):
            a = act_v[rows, j * 128 : (j + 1) * 128].astype(F32)
            total = total + a * a
        inverse = lax.rsqrt(jnp.sum(total, axis=-1, keepdims=True) / D + epsilon)
        wide = jnp.broadcast_to(inverse, (32, 128))
        inv_v[rows, :] = wide
        for j in range(32):
            a = act_v[rows, j * 128 : (j + 1) * 128].astype(F32)
            nrm[j, rows, :] = (a * wide * gain_row[:, j * 128 : (j + 1) * 128]).astype(BF)
        return 0

    lax.fori_loop(0, 16, norm, 0)
    load_cot.wait()

    halves = (1 - zh, zh)

    def block(quarter, i, s):
        return quarter * 8 + halves[i] * 4 + s * 2

    def send_a(n):
        i, s, t = n // 4, (n // 2) % 2, n % 2
        quarter = q if t == 0 else p1
        send(nrm.at[pl.ds(block(quarter, i, s), 2)], ra.at[n], ass.at[n], asem.at[n], dev_p1)

    for n in range(8):
        send_a(n)

    def product(n):
        i, s, t = n // 4, (n // 2) % 2, n % 2
        j = block(p2 if t == 0 else y, i, s)
        arrived(ra.at[n], asem.at[n])
        mine = jnp.concatenate([nrm[j], nrm[j + 1]], axis=1)
        theirs = jnp.concatenate([ra[n, 0], ra[n, 1]], axis=1)
        dims = (((0,), (0,)), ((), ()))
        total = lax.dot_general(mine, cot_v[...], dims, preferred_element_type=F32)
        total = total + lax.dot_general(theirs, rb[...], dims, preferred_element_type=F32)
        total = total * FACTOR
        if t == 0:
            ps[n // 2] = total.astype(BF)
            send(ps.at[n // 2], pr.at[n // 2], pss.at[n // 2], psem.at[n // 2], dev_p2)
        else:
            own[n // 2] = total

    def reduce_y(m):
        arrived(pr.at[m], psem.at[m])
        total = own[m] + pr[m].astype(F32)
        if m < 2:
            zs[m] = total.astype(BF)
            send(zs.at[m], zr.at[m], zss.at[m], zsem.at[m], dev_z4)
        else:
            own[m] = total

    out_copies = []

    def reduce_z(m):
        arrived(zr.at[m], zsem.at[m])
        wgo[m * 256 : (m + 1) * 256, :] = (own[2 + m] + zr[m].astype(F32)).astype(BF)
        cp = pltpu.make_async_copy(
            wgo.at[m * 256 : (m + 1) * 256], wg_o.at[0, m * 256 : (m + 1) * 256], osem.at[m]
        )
        cp.start()
        out_copies.append(cp)

    def grad_x():
        for i in range(3):
            arrived(g2r.at[i], g2sem.at[i])
        total = g1s[pl.ds(x * 4, 4)].astype(F32)
        for i in range(3):
            total = total + g2r[i].astype(F32)
        g2s[...] = total.astype(BF)
        for i in range(3):
            send(g2s.at[zlp[i]], g3r.at[i], g3ss.at[i], g3sem.at[i], dev_zl[i])

    def grad_z():
        for i in range(3):
            arrived(g3r.at[i], g3sem.at[i])
        total = g2s[zl].astype(F32)
        for i in range(3):
            total = total + g3r[i].astype(F32)
        delta = total / 32.0
        momentum_next = outer_beta * moment[...] + delta
        params_next = params[...] - outer_rate * (delta + outer_beta * momentum_next)
        mn_o[...] = momentum_next
        pn_o[...] = params_next
        wfull[y, zh, x, zl, c] = params_next.astype(BF)
        mine = wfull.at[y, zh, x, zl, c]
        for i in range(3):
            send(mine, mine, yss.at[i], ysem.at[i], dev_y[i])

    def wblock(vx, vz, core):
        return wfull.at[:, lax.div(vz, 4), vx, lax.rem(vz, 4), core]

    def got_z(k, sign):
        vz = lax.rem(z + 8 + sign * k, 8)
        ref = wblock(x, vz, c)
        if k > 0:
            arrived(ref, agsem.at[x, vz])
        if k == 0:
            send(ref, ref, zrs.at[0], agsem.at[x, vz], dev_zup)
            send(ref, ref, zrs.at[1], agsem.at[x, vz], dev_zdn)
        elif sign < 0 and k < 4:
            send(ref, ref, zrs.at[1 + k], agsem.at[x, vz], dev_zup)
        elif sign > 0 and k < 3:
            send(ref, ref, zrs.at[4 + k], agsem.at[x, vz], dev_zdn)
        send(ref, ref, xs.at[0, vz], agsem.at[x, vz], dev_x[0])
        send(ref, ref, xs.at[1, vz], agsem.at[x, vz], dev_x[2])
        send(ref, ref, sbs.at[x, vz], sbsem.at[x, vz], sibling)

    def got_x(d, k, sign):
        vz = lax.rem(z + 8 + sign * k, 8)
        vx = xp[d - 1]
        ref = wblock(vx, vz, c)
        arrived(ref, agsem.at[vx, vz])
        if d == 3 and k % 2 == 0:
            send(ref, ref, xs.at[2, vz], agsem.at[vx, vz], dev_x[0])
        if d == 1 and k % 2 == 1:
            send(ref, ref, xs.at[2, vz], agsem.at[vx, vz], dev_x[2])
        send(ref, ref, sbs.at[vx, vz], sbsem.at[vx, vz], sibling)

    group = {0: [(0, 1)], 1: [(1, -1), (1, 1)], 2: [(2, -1), (2, 1)], 3: [(3, -1), (3, 1)], 4: [(4, -1)]}

    def z_step(k):
        for kk, sign in group[k]:
            got_z(kk, sign)

    def x_step(k):
        for kk, sign in group[k]:
            got_x(1, kk, sign)
            got_x(3, kk, sign)

    def far_step(k):
        for kk, sign in group[k]:
            got_x(2, kk, sign)

    def gather_y():
        for i in range(3):
            ref = wfull.at[yp[2 - i], zh, x, zl, c]
            arrived(ref, ysem.at[i])

    def piece(d, vh, first):
        vx = lax.rem(x + d, 4)
        for vl in range(4):
            vz = vh * 4 + vl
            arrived(wblock(vx, vz, other), sbsem.at[vx, vz])
        w = wfull[:, vh, vx].reshape(512, K)
        lhs = jnp.concatenate([nrm[v * 8 + vh * 4 + vx] for v in range(4)], axis=1)
        part = jnp.dot(lhs, w, preferred_element_type=F32)
        acc[...] = part if first else acc[...] + part
        b = lax.dot_general(cot_v[...], w, (((1,), (1,)), ((), ())), preferred_element_type=F32)
        for v in range(4):
            back[v * 8 + vh * 4 + vx] = b[:, v * 128 : (v + 1) * 128]

    grad_x()
    arrived(rb, bsem)
    product(0)
    grad_z()
    product(1)
    product(2)
    gather_y()
    z_step(0)
    product(3)
    z_step(1)
    reduce_y(0)
    product(4)
    z_step(2)
    reduce_y(1)
    product(5)
    product(6)
    z_step(3)
    product(7)
    z_step(4)
    x_step(0)
    x_step(1)
    far_step(0)
    x_step(2)
    far_step(1)
    piece(0, zh, True)
    x_step(3)
    far_step(2)
    piece(0, 1 - zh, False)
    x_step(4)
    far_step(3)
    far_step(4)
    reduce_y(2)
    reduce_y(3)
    for d in (1, 3, 2):
        piece(d, zh, False)
        piece(d, 1 - zh, False)

    def finish(t, _):
        rows = pl.ds(pl.multiple_of(t * 64, 64), 64)
        a = acc[rows, :]
        prj[rows, :] = (a * FACTOR).astype(BF)
        dots = jnp.sum(a * cot_v[rows, :].astype(F32), axis=-1, keepdims=True)
        mrow[rows, :] = jnp.broadcast_to(dots * (FACTOR / D), (64, 128))
        return 0

    lax.fori_loop(0, 8, finish, 0)
    cp = pltpu.make_async_copy(prj, proj_o, osem.at[2])
    cp.start()
    out_copies.append(cp)

    gain_scaled = gain_row * FACTOR

    def grad_in(t, _):
        rows = pl.ds(pl.multiple_of(t * 64, 64), 64)
        inverse = inv_v[rows, :]
        m = mrow[rows, :] * inverse * inverse
        for j in range(32):
            cols = slice(j * 128, (j + 1) * 128)
            a = act_v[rows, cols].astype(F32)
            out = back[j, rows, :] * gain_scaled[:, cols] * inverse - a * m
            act_v[rows, cols] = out.astype(BF)
        pltpu.make_async_copy(act_v.at[rows], ig_o.at[rows], osem.at[3 + t]).start()
        return 0

    lax.fori_loop(0, 8, grad_in, 0)
    reduce_z(0)
    reduce_z(1)

    for t in range(8):
        rows = slice(t * 64, (t + 1) * 64)
        pltpu.make_async_copy(act_v.at[rows], ig_o.at[rows], osem.at[3 + t]).wait()
    for cp in out_copies:
        cp.wait()
    for cp in started:
        cp.wait_send()


def shards(fp8_codes, block_scales, outer_params, outer_momentum, activations, norm_gain, cotangent):
    anywhere = pl.BlockSpec(memory_space=pl.ANY)
    vmem = pl.BlockSpec(memory_space=pltpu.VMEM)
    dma = pltpu.SemaphoreType.DMA
    return pl.pallas_call(
        kernel,
        name="diloco",
        out_shape=(
            jax.ShapeDtypeStruct((T, K), BF),
            jax.ShapeDtypeStruct((T, D), BF),
            jax.ShapeDtypeStruct((1, T, K), BF),
            jax.ShapeDtypeStruct((16, K), F32),
            jax.ShapeDtypeStruct((16, K), F32),
        ),
        in_specs=[anywhere, vmem, vmem, vmem, anywhere, vmem, anywhere],
        out_specs=(anywhere, anywhere, anywhere, vmem, vmem),
        scratch_shapes=[
            pltpu.VMEM((512, K), jnp.int32),
            pltpu.VMEM((T, D), BF),
            pltpu.VMEM((T, K), BF),
            pltpu.VMEM((32, T, 128), BF),
            pltpu.VMEM((T, 128), F32),
            pltpu.VMEM((2, 16, 16, K), BF),
            pltpu.VMEM((16, 16, K), BF),
            pltpu.VMEM((16, 16, K), BF),
            pltpu.VMEM((3, 4, 16, K), BF),
            pltpu.VMEM((4, 16, K), BF),
            pltpu.VMEM((3, 16, K), BF),
            pltpu.VMEM((4, 2, 4, 4, 2, 16, K), BF),
            pltpu.VMEM((T, K), F32),
            pltpu.VMEM((32, T, 128), F32),
            pltpu.VMEM((T, K), BF),
            pltpu.VMEM((8, 2, T, 128), BF),
            pltpu.VMEM((4, 256, K), BF),
            pltpu.VMEM((4, 256, K), F32),
            pltpu.VMEM((4, 256, K), BF),
            pltpu.VMEM((2, 256, K), BF),
            pltpu.VMEM((2, 256, K), BF),
            pltpu.VMEM((T, K), BF),
            pltpu.VMEM((T, K), BF),
            pltpu.VMEM((T, 128), F32),
            dma((3,)),
            dma((11,)),
            dma,
            dma((8,)),
            dma((4,)),
            dma((2,)),
            dma,
            dma((3,)),
            dma((3,)),
            dma((3,)),
            dma((4, 8)),
            dma((4, 8)),
            dma,
            dma((8,)),
            dma((4,)),
            dma((2,)),
            dma,
            dma((3,)),
            dma((3,)),
            dma((3,)),
            dma((7,)),
            dma((3, 8)),
            dma((4, 8)),
        ],
        compiler_params=pltpu.CompilerParams(
            collective_id=0, has_side_effects=True, vmem_limit_bytes=60 * 1024 * 1024
        ),
        cost_estimate=pl.CostEstimate(flops=13 * 10**9, bytes_accessed=14 * 2**20, transcendentals=0),
    )(
        fp8_codes, block_scales, outer_params, outer_momentum, activations,
        norm_gain.reshape(1, D), cotangent,
    )


def solution(mesh):
    in_specs = (
        P("replica", "fsdp", None),
        P("replica", None, "fsdp"),
        P(("fsdp", "replica"), None),
        P(("fsdp", "replica"), None),
        P(("replica", "fsdp"), None),
        P(),
        P(("replica", "fsdp"), None),
    )
    out_specs = (
        P(("replica", "fsdp"), None),
        P(("replica", "fsdp"), None),
        P("replica", "fsdp", None),
        P(("fsdp", "replica"), None),
        P(("fsdp", "replica"), None),
    )
    return jax.shard_map(shards, mesh=mesh, in_specs=in_specs, out_specs=out_specs, check_vma=False)
```

time: 789 us -> 163 us (0.21)
  the two profiles are of different devices: /device:TPU:1 before, /device:TPU:66 now
where the time goes in v1:
time: 163 us
  Pallas kernels  152 us (93%)
  local copies, waits for them, and re-layouts  10.6 us (7%)
    pallas_call x1, Pallas kernels, shards(): pl.pallas_call(kernel, name='diloco', out_shape=(jax.ShapeDtypeStruct((T,...  152 us
    unnamed x11, local copies, waits for them, and re-layouts  9.3 us

profile of v1, /device:TPU:66, one launch (start us, length us, event | category | flops | bytes accessed | tf_op | source)
XLA Modules:
  0.0 162.9 jit_solution(12703815402140965251)
XLA Ops:
  0.6 1.3 reshape.13.gain
  1.9 151.6 %diloco.1 = (bf16[512,1024]{1,0:T(8,128)(2,1)}, bf16[512,4096]{1,0:T(8,128)(2,1)}, bf16[1,512,1024]{2,1,0:T(8,128)(2,1)}, f32[16,1024]{1,0:T(8,128)}, f32[16,1024]{1,0:T(8,128)}) custom-call(s32[1,512,1024]{2,1,0:T(8,128)} %codes.1, s32[1,8,512]{2,1,0:T(8,128)} %scales.1, f32[16,1024]{1,0:T(8,128)} %params.1, f32[16,1024]{1,0:T(8,128)} %moment.1, ...), custom_call_target="tpu_custom_call" | custom-call | flops 12999999488 | bytes 14680064 | tf_op jit(solution)/shard_map/diloco/pallas_call | solution.py:357
  153.6 2.3 %copy.17 = bf16[512,1024]{1,0:T(8,128)(2,1)} copy(bf16[512,1024]{1,0:T(8,128)(2,1)} %get-tuple-element.10) | data formatting | bytes 2097152
  155.9 0.0 copy-start
  155.9 0.0 copy-start.2
  155.9 0.0 copy-start.1
  155.9 4.8 %copy.18 = bf16[512,4096]{1,0:T(8,128)(2,1)} copy(bf16[512,4096]{1,0:T(8,128)(2,1)} %get-tuple-element.11) | data formatting | bytes 8388608
  160.7 0.0 copy-done
  160.7 1.0 copy.19
  161.6 0.0 copy-done.2
  161.6 0.6 copy.20
  162.3 0.0 copy-done.1
  162.3 0.6 copy.21
Async XLA Ops:
  155.9 4.8 %copy-start = (bf16[1,512,1024]{2,1,0:T(8,128)(2,1)S(1)}, bf16[1,512,1024]{2,1,0:T(8,128)(2,1)}, u32[]{:S(2)}) copy-start(bf16[1,512,1024]{2,1,0:T(8,128)(2,1)} %get-tuple-element.12) | copy-start | bytes 3145732
  155.9 5.8 %copy-start.2 = (f32[16,1024]{1,0:T(8,128)S(1)}, f32[16,1024]{1,0:T(8,128)}, u32[]{:S(2)}) copy-start(f32[16,1024]{1,0:T(8,128)} %get-tuple-element.13) | copy-start | bytes 196612
  155.9 6.4 %copy-start.1 = (f32[16,1024]{1,0:T(8,128)S(1)}, f32[16,1024]{1,0:T(8,128)}, u32[]{:S(2)}) copy-start(f32[16,1024]{1,0:T(8,128)} %get-tuple-element.14) | copy-start | bytes 196612

commit v2 on v1

v2 whole, which is shorter than its diff:
```python
import functools

import jax
import jax.numpy as jnp
from jax import lax
from jax.experimental import pallas as pl
from jax.experimental.pallas import tpu as pltpu
from jax.sharding import PartitionSpec as P

outer_rate = 0.7
outer_beta = 0.9
epsilon = 1e-05
BF = jnp.bfloat16
F32 = jnp.float32
MESH = pl.DeviceIdType.MESH
D = 4096
T = 512
K = 1024
FACTOR = D ** (-0.5)


def device(x, y, z, c):
    return ((x * 4 + lax.rem(z, 4)) * 2 + c, y * 2 + lax.div(z, 4))


def kernel(
    codes, scales, params, moment, act, gain, cot,
    act_v, back, prj, wgo, inv_v, mrow, pn_o, mn_o,
    codes_v, cot_v, nrm, dec, g1r, g1s, g2r, g2s, g3r, wfull, acc,
    rb, ra, ps, own, pr, zs, zr,
    lsem, bsem, asem, psem, zsem, gsem, g2sem, g3sem, zgsem, ygsem, xgsem, sbsem,
    bss, ass, pss, zss, gss, g2ss, g3ss, zgs, ygs, xgs, sbs,
):
    r = lax.axis_index("replica")
    f = lax.axis_index("fsdp")
    x, zl, c = lax.div(r, 8), lax.rem(lax.div(r, 2), 4), lax.rem(r, 2)
    y, zh = lax.div(f, 2), lax.rem(f, 2)
    z = zh * 4 + zl
    other = 1 - c
    swap = y + 1 - 2 * lax.rem(y, 2)
    p1 = c * (3 - y) + other * swap
    p2 = c * swap + other * (3 - y)
    q = lax.rem(y + 2, 4)
    sibling = device(x, y, z, other)
    dev_p1, dev_p2 = device(x, p1, z, c), device(x, p2, z, c)
    xp = [lax.rem(x + d, 4) for d in (1, 2, 3)]
    zlp = [lax.rem(zl + d, 4) for d in (1, 2, 3)]
    yp = [lax.rem(y + d, 4) for d in (1, 2, 3)]
    zp = [lax.rem(z + d, 8) for d in range(1, 8)]
    dev_x = [device(v, y, z, c) for v in xp]
    dev_zl = [device(x, y, zh * 4 + v, c) for v in zlp]
    dev_y = [device(x, v, z, c) for v in yp]
    dev_z = [device(x, y, v, c) for v in zp]
    dev_z4 = dev_z[3]

    started = []

    def send(src, dst, ss, rs, to):
        cp = pltpu.make_async_remote_copy(
            src_ref=src, dst_ref=dst, send_sem=ss, recv_sem=rs, device_id=to, device_id_type=MESH
        )
        cp.start()
        started.append(cp)

    def arrived(dst, rs):
        pltpu.make_async_remote_copy(
            src_ref=dst, dst_ref=dst, send_sem=bss, recv_sem=rs, device_id=sibling, device_id_type=MESH
        ).wait_recv()

    load_codes = pltpu.make_async_copy(codes.at[0], codes_v, lsem.at[0])
    load_act = pltpu.make_async_copy(act, act_v, lsem.at[1])
    load_cot = pltpu.make_async_copy(cot, cot_v, lsem.at[2])
    load_codes.start()
    load_act.start()
    load_cot.start()

    barrier = pltpu.get_barrier_semaphore()
    friends = [sibling, *dev_x, *dev_y, *dev_z]
    for to in friends:
        pl.semaphore_signal(barrier, inc=1, device_id=to, device_id_type=MESH)

    factors = jnp.exp2((scales[0] - 127).astype(F32)).astype(BF)
    spread = (
        lax.broadcasted_iota(jnp.int32, (8, K), 1) // 128 == lax.broadcasted_iota(jnp.int32, (8, K), 0)
    ).astype(F32).astype(BF)
    acc[...] = lax.dot_general(factors, spread, (((0,), (0,)), ((), ())), preferred_element_type=F32)
    load_codes.wait()

    def decode_half(which):
        def step(g, _):
            rows = pl.ds(pl.multiple_of(g * 32 + which * 16, 16), 16)
            code = codes_v[rows, :]
            field = (code >> 3) & 15
            low = code & 7
            whole = jnp.where(field > 0, low + 8, low * 2) << field
            value = whole.astype(F32) * (acc[rows, :] * (2.0**-10))
            dec[which, g] = jnp.where(code >= 128, -value, value).astype(BF)
            return 0

        lax.fori_loop(0, 16, step, 0)

    decode_half(other)
    pl.semaphore_wait(barrier, len(friends))
    send(cot, rb, bss, bsem, dev_p1)
    send(dec.at[other], g1r, gss, gsem, sibling)
    decode_half(c)
    arrived(g1r, gsem)

    def sum_one(g, _):
        g1s[g] = (dec[c, g].astype(F32) + g1r[g].astype(F32)).astype(BF)
        return 0

    lax.fori_loop(0, 16, sum_one, 0)
    for i in range(3):
        send(g1s.at[pl.ds(xp[i] * 4, 4)], g2r.at[i], g2ss.at[i], g2sem.at[i], dev_x[i])

    load_act.wait()
    gain_row = gain[...].astype(F32)

    def norm(t, _):
        rows = pl.ds(pl.multiple_of(t * 32, 32), 32)
        total = jnp.zeros((32, 128), F32)
        for j in range(32):
            a = act_v[rows, j * 128 : (j + 1) * 128].astype(F32)
            total = total + a * a
        inverse = lax.rsqrt(jnp.sum(total, axis=-1, keepdims=True) / D + epsilon)
        wide = jnp.broadcast_to(inverse, (32, 128))
        inv_v[rows, :] = wide
        for j in range(32):
            a = act_v[rows, j * 128 : (j + 1) * 128].astype(F32)
            nrm[j, rows, :] = (a * wide * gain_row[:, j * 128 : (j + 1) * 128]).astype(BF)
        return 0

    lax.fori_loop(0, 16, norm, 0)
    load_cot.wait()

    halves = (1 - zh, zh)
    chunks = ((0, 0, 1), (0, 1, 1), (0, 2, 2), (1, 0, 2), (1, 2, 2))

    def send_a(n):
        i, first, count = chunks[n // 2]
        quarter = (q, p1)[n % 2]
        src = nrm.at[pl.ds(quarter * 8 + halves[i] * 4 + first, count)]
        dst = ra.at[n % 2, i * 4 + first : i * 4 + first + count]
        send(src, dst, ass.at[n], asem.at[n], dev_p1)

    send_a(0)
    send_a(1)

    def product(n):
        m = n // 2
        i, first, count = chunks[m]
        low = i * 4 + first
        arrived(ra.at[n % 2, low : low + count], asem.at[n])
        if n < 8:
            send_a(n + 2)
        j = (p2, y)[n % 2] * 8 + halves[i] * 4 + first
        mine = jnp.concatenate([nrm[j + b] for b in range(count)], axis=1)
        theirs = jnp.concatenate([ra[n % 2, low + b] for b in range(count)], axis=1)
        dims = (((0,), (0,)), ((), ()))
        total = lax.dot_general(mine, cot_v[...], dims, preferred_element_type=F32)
        total = total + lax.dot_general(theirs, rb[...], dims, preferred_element_type=F32)
        total = total * FACTOR
        rows = slice(low * 128, (low + count) * 128)
        if n % 2 == 0:
            ps[rows, :] = total.astype(BF)
            send(ps.at[rows], pr.at[rows], pss.at[m], psem.at[m], dev_p2)
        else:
            own[rows, :] = total

    def reduce_y(m):
        i, first, count = chunks[m]
        rows = slice((i * 4 + first) * 128, (i * 4 + first + count) * 128)
        arrived(pr.at[rows], psem.at[m])
        total = own[rows, :] + pr[rows, :].astype(F32)
        if i == 0:
            zs[rows, :] = total.astype(BF)
            send(zs.at[rows], zr.at[rows], zss.at[m], zsem.at[m], dev_z4)
        else:
            own[rows, :] = total

    def reduce_z(m):
        _, first, count = chunks[m]
        rows = slice(first * 128, (first + count) * 128)
        arrived(zr.at[rows], zsem.at[m])
        summed = own[512 + first * 128 : 512 + (first + count) * 128, :]
        wgo[rows, :] = (summed + zr[rows, :].astype(F32)).astype(BF)

    def grad_x():
        for i in range(3):
            arrived(g2r.at[i], g2sem.at[i])
        total = g1s[pl.ds(x * 4, 4)].astype(F32)
        for i in range(3):
            total = total + g2r[i].astype(F32)
        g2s[...] = total.astype(BF)
        for i in range(3):
            send(g2s.at[zlp[i]], g3r.at[i], g3ss.at[i], g3sem.at[i], dev_zl[i])

    def grad_z():
        for i in range(3):
            arrived(g3r.at[i], g3sem.at[i])
        total = g2s[zl].astype(F32)
        for i in range(3):
            total = total + g3r[i].astype(F32)
        delta = total / 32.0
        momentum_next = outer_beta * moment[...] + delta
        params_next = params[...] - outer_rate * (delta + outer_beta * momentum_next)
        mn_o[...] = momentum_next
        pn_o[...] = params_next
        wfull[y, zh, x, zl, c] = params_next.astype(BF)
        mine = wfull.at[y, zh, x, zl, c]
        for i in range(7):
            send(mine, mine, zgs.at[i], zgsem.at[i], dev_z[i])

    def gather_z():
        for i in range(7):
            v = lax.rem(z + 7 - i, 8)
            arrived(wfull.at[y, lax.div(v, 4), x, lax.rem(v, 4), c], zgsem.at[i])

    def wblock(vx, vy, core):
        return wfull.at[vy, :, vx, :, core]

    def whalf(vx, vy, half):
        return wfull.at[vy, half, vx, :, c]

    def row_of(d):
        return lax.rem(y + d, 4)

    def y_step(d):
        vy = row_of(d)
        ref = wblock(x, vy, c)
        if d == 0:
            send(ref, ref, ygs.at[0], ygsem.at[vy, 0], dev_y[0])
            send(ref, ref, ygs.at[1], ygsem.at[vy, 0], dev_y[2])
        elif d == 3:
            arrived(ref, ygsem.at[vy, 0])
            send(whalf(x, vy, 0), whalf(x, vy, 0), ygs.at[2], ygsem.at[vy, 0], dev_y[0])
        elif d == 1:
            arrived(ref, ygsem.at[vy, 0])
            send(whalf(x, vy, 1), whalf(x, vy, 1), ygs.at[3], ygsem.at[vy, 1], dev_y[2])
        else:
            arrived(whalf(x, vy, 0), ygsem.at[vy, 0])
            arrived(whalf(x, vy, 1), ygsem.at[vy, 1])
        send(ref, ref, xgs.at[vy, 0], xgsem.at[x, vy, 0], dev_x[0])
        send(ref, ref, xgs.at[vy, 1], xgsem.at[x, vy, 0], dev_x[2])
        send(ref, ref, sbs.at[x, vy], sbsem.at[x, vy], sibling)

    def x_near(d):
        vy = row_of(d)
        for dx, half, to in ((3, 0, 0), (1, 1, 2)):
            vx = xp[dx - 1]
            ref = wblock(vx, vy, c)
            arrived(ref, xgsem.at[vx, vy, 0])
            part = whalf(vx, vy, half)
            send(part, part, xgs.at[vy, 2 + half], xgsem.at[vx, vy, half], dev_x[to])
            send(ref, ref, sbs.at[vx, vy], sbsem.at[vx, vy], sibling)

    def x_far(d):
        vy = row_of(d)
        vx = xp[1]
        for half in range(2):
            arrived(whalf(vx, vy, half), xgsem.at[vx, vy, half])
        ref = wblock(vx, vy, c)
        send(ref, ref, sbs.at[vx, vy], sbsem.at[vx, vy], sibling)

    def piece(dx, dy, first=False):
        vx, vy = lax.rem(x + dx, 4), row_of(dy)
        arrived(wblock(vx, vy, other), sbsem.at[vx, vy])
        w = wfull[vy, :, vx].reshape(256, K)
        j = vy * 8 + vx
        lhs = jnp.concatenate([nrm[j], nrm[j + 4]], axis=1)
        part = jnp.dot(lhs, w, preferred_element_type=F32)
        acc[...] = part if first else acc[...] + part
        b = lax.dot_general(cot_v[...], w, (((1,), (1,)), ((), ())), preferred_element_type=F32)
        back[j] = b[:, :128]
        back[j + 4] = b[:, 128:]

    grad_x()
    arrived(rb, bsem)
    product(0)
    product(1)
    grad_z()
    product(2)
    reduce_y(0)
    product(3)
    product(4)
    reduce_y(1)
    gather_z()
    y_step(0)
    product(5)
    piece(0, 0, True)
    x_near(0)
    reduce_y(2)
    product(6)
    y_step(3)
    y_step(1)
    product(7)
    x_far(0)
    piece(1, 0)
    piece(3, 0)
    x_near(3)
    reduce_y(3)
    x_near(1)
    product(8)
    y_step(2)
    piece(2, 0)
    piece(0, 3)
    piece(0, 1)
    product(9)
    x_far(3)
    x_far(1)
    for dy in (3, 1):
        piece(1, dy)
        piece(3, dy)
    x_near(2)
    piece(0, 2)
    piece(2, 3)
    piece(2, 1)
    x_far(2)
    reduce_y(4)
    piece(1, 2)
    piece(3, 2)
    piece(2, 2)

    def finish(t, _):
        rows = pl.ds(pl.multiple_of(t * 64, 64), 64)
        a = acc[rows, :]
        prj[rows, :] = (a * FACTOR).astype(BF)
        dots = jnp.sum(a * cot_v[rows, :].astype(F32), axis=-1, keepdims=True)
        mrow[rows, :] = jnp.broadcast_to(dots * (FACTOR / D), (64, 128))
        return 0

    lax.fori_loop(0, 8, finish, 0)
    for m in range(3):
        reduce_z(m)

    for cp in started:
        cp.wait_send()


def finish_kernel(act_v, back, prj, wgo, inv_v, mrow, gain, pn, mn, proj_o, ig_o, wg_o, pn_o, mn_o, grad, sem):
    copies = [
        pltpu.make_async_copy(prj, proj_o, sem.at[8]),
        pltpu.make_async_copy(wgo, wg_o.at[0], sem.at[9]),
        pltpu.make_async_copy(pn, pn_o, sem.at[10]),
        pltpu.make_async_copy(mn, mn_o, sem.at[11]),
    ]
    for cp in copies:
        cp.start()
    gain_scaled = gain[...].astype(F32) * FACTOR

    def grad_in(t, _):
        rows = pl.ds(pl.multiple_of(t * 64, 64), 64)
        inverse = inv_v[rows, :]
        m = mrow[rows, :] * inverse * inverse
        for j in range(32):
            cols = slice(j * 128, (j + 1) * 128)
            a = act_v[rows, cols].astype(F32)
            out = back[j, rows, :] * gain_scaled[:, cols] * inverse - a * m
            grad[rows, cols] = out.astype(BF)
        pltpu.make_async_copy(grad.at[rows], ig_o.at[rows], sem.at[t]).start()
        return 0

    lax.fori_loop(0, 8, grad_in, 0)
    for t in range(8):
        rows = slice(t * 64, (t + 1) * 64)
        pltpu.make_async_copy(grad.at[rows], ig_o.at[rows], sem.at[t]).wait()
    for cp in copies:
        cp.wait()


def shards(fp8_codes, block_scales, outer_params, outer_momentum, activations, norm_gain, cotangent):
    anywhere = pl.BlockSpec(memory_space=pl.ANY)
    vmem = pl.BlockSpec(memory_space=pltpu.VMEM)
    dma = pltpu.SemaphoreType.DMA
    gain_row = norm_gain.reshape(1, D)
    act_v, back, prj, wgo, inv_v, mrow, pn, mn = pl.pallas_call(
        kernel,
        name="exchange",
        out_shape=(
            pltpu.VMEM((T, D), BF),
            pltpu.VMEM((32, T, 128), F32),
            pltpu.VMEM((T, K), BF),
            pltpu.VMEM((T, K), BF),
            pltpu.VMEM((T, 128), F32),
            pltpu.VMEM((T, 128), F32),
            pltpu.VMEM((16, K), F32),
            pltpu.VMEM((16, K), F32),
        ),
        in_specs=[anywhere, vmem, vmem, vmem, anywhere, vmem, anywhere],
        out_specs=(vmem,) * 8,
        scratch_shapes=[
            pltpu.VMEM((512, K), jnp.int32),
            pltpu.VMEM((T, K), BF),
            pltpu.VMEM((32, T, 128), BF),
            pltpu.VMEM((2, 16, 16, K), BF),
            pltpu.VMEM((16, 16, K), BF),
            pltpu.VMEM((16, 16, K), BF),
            pltpu.VMEM((3, 4, 16, K), BF),
            pltpu.VMEM((4, 16, K), BF),
            pltpu.VMEM((3, 16, K), BF),
            pltpu.VMEM((4, 2, 4, 4, 2, 16, K), BF),
            pltpu.VMEM((T, K), F32),
            pltpu.VMEM((T, K), BF),
            pltpu.VMEM((2, 8, T, 128), BF),
            pltpu.VMEM((1024, K), BF),
            pltpu.VMEM((1024, K), F32),
            pltpu.VMEM((1024, K), BF),
            pltpu.VMEM((512, K), BF),
            pltpu.VMEM((512, K), BF),
            dma((3,)),
            dma,
            dma((10,)),
            dma((5,)),
            dma((3,)),
            dma,
            dma((3,)),
            dma((3,)),
            dma((7,)),
            dma((4, 2)),
            dma((4, 4, 2)),
            dma((4, 4)),
            dma,
            dma((10,)),
            dma((5,)),
            dma((3,)),
            dma,
            dma((3,)),
            dma((3,)),
            dma((7,)),
            dma((4,)),
            dma((4, 4)),
            dma((4, 4)),
        ],
        compiler_params=pltpu.CompilerParams(
            collective_id=0, has_side_effects=True, vmem_limit_bytes=45 * 1024 * 1024
        ),
        cost_estimate=pl.CostEstimate(flops=13 * 10**9, bytes_accessed=14 * 2**20, transcendentals=0),
    )(
        fp8_codes, block_scales, outer_params, outer_momentum, activations,
        gain_row, cotangent,
    )
    return pl.pallas_call(
        finish_kernel,
        name="finish",
        out_shape=(
            jax.ShapeDtypeStruct((T, K), BF),
            jax.ShapeDtypeStruct((T, D), BF),
            jax.ShapeDtypeStruct((1, T, K), BF),
            jax.ShapeDtypeStruct((16, K), F32),
            jax.ShapeDtypeStruct((16, K), F32),
        ),
        in_specs=[vmem] * 9,
        out_specs=(anywhere,) * 5,
        scratch_shapes=[pltpu.VMEM((T, D), BF), dma((12,))],
        compiler_params=pltpu.CompilerParams(vmem_limit_bytes=16 * 1024 * 1024),
    )(act_v, back, prj, wgo, inv_v, mrow, gain_row, pn, mn)


def solution(mesh):
    in_specs = (
        P("replica", "fsdp", None),
        P("replica", None, "fsdp"),
        P(("fsdp", "replica"), None),
        P(("fsdp", "replica"), None),
        P(("replica", "fsdp"), None),
        P(),
        P(("replica", "fsdp"), None),
    )
    out_specs = (
        P(("replica", "fsdp"), None),
        P(("replica", "fsdp"), None),
        P("replica", "fsdp", None),
        P(("fsdp", "replica"), None),
        P(("fsdp", "replica"), None),
    )
    return jax.shard_map(shards, mesh=mesh, in_specs=in_specs, out_specs=out_specs, check_vma=False)
```

time: 163 us -> 95.2 us (0.58)
  the two profiles are of different devices: /device:TPU:66 before, /device:TPU:1 now
where the time goes in v2:
time: 95.2 us; the launch traced here: 95 us
  Pallas kernels  92.9 us (98%)
  local copies, waits for them, and re-layouts  1.32 us (1%)
    pallas_call x1, Pallas kernels, shards(): pl.pallas_call(kernel, name='exchange', out_shape=(pltpu.VMEM((T, D), BF)...  90.1 us
    pallas_call x1, Pallas kernels, shards(): pl.pallas_call(finish_kernel, name='finish', out_shape=(jax.ShapeDtypeStr...  2.8 us

profile of v2, /device:TPU:1, one launch (start us, length us, event | category | flops | bytes accessed | tf_op | source)
XLA Modules:
  0.0 95.0 jit_solution(12641995699774559261)
XLA Ops:
  0.6 1.3 %reshape.13.gain = bf16[1,4096]{1,0:T(2,128)(2,1)} reshape(bf16[4096]{0:T(1024)(128)(2,1)} %param.12) | data formatting | bytes 16384 | tf_op jit(solution)/shard_map/reshape | solution.py:376
  1.9 0.0 copy-start
  1.9 90.1 %exchange.1 = (bf16[512,4096]{1,0:T(8,128)(2,1)S(1)}, f32[32,512,128]{2,1,0:T(8,128)S(1)}, bf16[512,1024]{1,0:T(8,128)(2,1)S(1)}, bf16[512,1024]{1,0:T(8,128)(2,...) custom-call(s32[1,512,1024]{2,1,0:T(8,128)} %codes.1, ...), custom_call_target="tpu_custom_call" | custom-call | flops 12999999488 | bytes 14680064 | tf_op jit(solution)/shard_map/exchange/pallas_call | solution.py:377
  92.1 0.0 copy-done
  92.1 2.8 %finish.1 = (bf16[512,1024]{1,0:T(8,128)(2,1)}, bf16[512,4096]{1,0:T(8,128)(2,1)}, bf16[1,512,1024]{2,1,0:T(8,128)(2,1)}, f32[16,1024]{1,0:T(8,128)}, f32[16,1024]{1,0:T(8,128)}) custom-call(bf16[512,4096]{1,0:T(8,128)(2,1)S(1)} %get-tuple-element.13.act_v, f32[32,512,128]{2,1,0:T(8,128)S(1)} %get-tuple-element.14.back, ...), custom_call_target="tpu_custom_call" | custom-call | tf_op jit(solution)/shard_map/finish/pallas_call | solution.py:443
Async XLA Ops:
  1.9 90.1 %copy-start = (bf16[1,4096]{1,0:T(2,128)(2,1)S(1)}, bf16[1,4096]{1,0:T(2,128)(2,1)}, u32[]{:S(2)}) copy-start(bf16[1,4096]{1,0:T(2,128)(2,1)} %reshape.13.gain) | copy-start | bytes 24580

commit v3 on v2

--- a/solution.py
+++ b/solution.py
@@ -64,7 +64,7 @@
 
     def arrived(dst, rs):
         pltpu.make_async_remote_copy(
-            src_ref=dst, dst_ref=dst, send_sem=bss, recv_sem=rs, device_id=sibling, device_id_type=MESH
+            src_ref=dst, dst_ref=dst, send_sem=bss.at[0], recv_sem=rs, device_id=sibling, device_id_type=MESH
         ).wait_recv()
 
     load_codes = pltpu.make_async_copy(codes.at[0], codes_v, lsem.at[0])
@@ -78,6 +78,13 @@
     friends = [sibling, *dev_x, *dev_y, *dev_z]
     for to in friends:
         pl.semaphore_signal(barrier, inc=1, device_id=to, device_id_type=MESH)
+    pl.semaphore_wait(barrier, len(friends))
+
+    def send_b(k):
+        cols = slice(k * 512, (k + 1) * 512)
+        send(cot.at[:, cols], rb.at[:, cols], bss.at[k], bsem.at[k], dev_p1)
+
+    send_b(0)
 
     factors = jnp.exp2((scales[0] - 127).astype(F32)).astype(BF)
     spread = (
@@ -100,8 +107,6 @@
         lax.fori_loop(0, 16, step, 0)
 
     decode_half(other)
-    pl.semaphore_wait(barrier, len(friends))
-    send(cot, rb, bss, bsem, dev_p1)
     send(dec.at[other], g1r, gss, gsem, sibling)
     decode_half(c)
     arrived(g1r, gsem)
@@ -115,7 +120,7 @@
         send(g1s.at[pl.ds(xp[i] * 4, 4)], g2r.at[i], g2ss.at[i], g2sem.at[i], dev_x[i])
 
     load_act.wait()
-    gain_row = gain[...].astype(F32)
+    gain_row = gain[...].astype(F32).reshape(1, D)
 
     def norm(t, _):
         rows = pl.ds(pl.multiple_of(t * 32, 32), 32)
@@ -135,56 +140,63 @@
     load_cot.wait()
 
     halves = (1 - zh, zh)
-    chunks = ((0, 0, 1), (0, 1, 1), (0, 2, 2), (1, 0, 2), (1, 2, 2))
-
-    def send_a(n):
-        i, first, count = chunks[n // 2]
-        quarter = (q, p1)[n % 2]
-        src = nrm.at[pl.ds(quarter * 8 + halves[i] * 4 + first, count)]
-        dst = ra.at[n % 2, i * 4 + first : i * 4 + first + count]
-        send(src, dst, ass.at[n], asem.at[n], dev_p1)
-
-    send_a(0)
-    send_a(1)
-
-    def product(n):
-        m = n // 2
-        i, first, count = chunks[m]
+    left, right, whole = slice(0, 512), slice(512, K), slice(0, K)
+    chunks = (
+        (0, 0, 1, left), (0, 1, 1, left), (0, 2, 2, left), (0, 0, 2, right), (0, 2, 2, right),
+        (1, 0, 2, whole), (1, 2, 2, whole),
+    )
+
+    def send_a(m, t):
+        i, first, count, _ = chunks[m]
+        src = nrm.at[pl.ds((q, p1)[t] * 8 + halves[i] * 4 + first, count)]
+        dst = ra.at[t, i * 4 + first : i * 4 + first + count]
+        send(src, dst, ass.at[m, t], asem.at[m, t], dev_p1)
+
+    send_a(0, 0)
+    send_a(0, 1)
+
+    def product(m, t):
+        i, first, count, cols = chunks[m]
         low = i * 4 + first
-        arrived(ra.at[n % 2, low : low + count], asem.at[n])
-        if n < 8:
-            send_a(n + 2)
-        j = (p2, y)[n % 2] * 8 + halves[i] * 4 + first
+        if m not in (3, 4):
+            arrived(ra.at[t, low : low + count], asem.at[m, t])
+        if m < 2:
+            send_a(m + 1, t)
+        if m == 3 and t == 0:
+            arrived(rb.at[:, right], bsem.at[1])
+        if m == 4:
+            send_a(6, t)
+        j = (p2, y)[t] * 8 + halves[i] * 4 + first
         mine = jnp.concatenate([nrm[j + b] for b in range(count)], axis=1)
-        theirs = jnp.concatenate([ra[n % 2, low + b] for b in range(count)], axis=1)
+        theirs = jnp.concatenate([ra[t, low + b] for b in range(count)], axis=1)
         dims = (((0,), (0,)), ((), ()))
-        total = lax.dot_general(mine, cot_v[...], dims, preferred_element_type=F32)
-        total = total + lax.dot_general(theirs, rb[...], dims, preferred_element_type=F32)
+        total = lax.dot_general(mine, cot_v[:, cols], dims, preferred_element_type=F32)
+        total = total + lax.dot_general(theirs, rb[:, cols], dims, preferred_element_type=F32)
         total = total * FACTOR
         rows = slice(low * 128, (low + count) * 128)
-        if n % 2 == 0:
-            ps[rows, :] = total.astype(BF)
-            send(ps.at[rows], pr.at[rows], pss.at[m], psem.at[m], dev_p2)
+        if t == 0:
+            ps[rows, cols] = total.astype(BF)
+            send(ps.at[rows, cols], pr.at[rows, cols], pss.at[m], psem.at[m], dev_p2)
         else:
-            own[rows, :] = total
+            own[rows, cols] = total
 
     def reduce_y(m):
-        i, first, count = chunks[m]
+        i, first, count, cols = chunks[m]
         rows = slice((i * 4 + first) * 128, (i * 4 + first + count) * 128)
-        arrived(pr.at[rows], psem.at[m])
-        total = own[rows, :] + pr[rows, :].astype(F32)
+        arrived(pr.at[rows, cols], psem.at[m])
+        total = own[rows, cols] + pr[rows, cols].astype(F32)
         if i == 0:
-            zs[rows, :] = total.astype(BF)
-            send(zs.at[rows], zr.at[rows], zss.at[m], zsem.at[m], dev_z4)
+            zs[rows, cols] = total.astype(BF)
+            send(zs.at[rows, cols], zr.at[rows, cols], zss.at[m], zsem.at[m], dev_z4)
         else:
-            own[rows, :] = total
+            own[rows, cols] = total
 
     def reduce_z(m):
-        _, first, count = chunks[m]
+        _, first, count, cols = chunks[m]
         rows = slice(first * 128, (first + count) * 128)
-        arrived(zr.at[rows], zsem.at[m])
-        summed = own[512 + first * 128 : 512 + (first + count) * 128, :]
-        wgo[rows, :] = (summed + zr[rows, :].astype(F32)).astype(BF)
+        arrived(zr.at[rows, cols], zsem.at[m])
+        summed = own[512 + first * 128 : 512 + (first + count) * 128, cols]
+        wgo[rows, cols] = (summed + zr[rows, cols].astype(F32)).astype(BF)
 
     def grad_x():
         for i in range(3):
@@ -275,49 +287,59 @@
         back[j] = b[:, :128]
         back[j + 4] = b[:, 128:]
 
+    arrived(rb.at[:, left], bsem.at[0])
+    product(0, 0)
     grad_x()
-    arrived(rb, bsem)
-    product(0)
-    product(1)
+    product(0, 1)
+    product(1, 0)
+    product(1, 1)
     grad_z()
-    product(2)
-    reduce_y(0)
-    product(3)
-    product(4)
-    reduce_y(1)
+    product(2, 0)
+    product(2, 1)
     gather_z()
     y_step(0)
-    product(5)
+    reduce_y(0)
+    reduce_y(1)
+    reduce_y(2)
     piece(0, 0, True)
     x_near(0)
-    reduce_y(2)
-    product(6)
     y_step(3)
     y_step(1)
-    product(7)
+    send_b(1)
+    send_a(5, 0)
+    send_a(5, 1)
     x_far(0)
     piece(1, 0)
     piece(3, 0)
+    y_step(2)
+    product(3, 0)
+    product(3, 1)
     x_near(3)
+    product(4, 0)
+    product(4, 1)
     reduce_y(3)
     x_near(1)
-    product(8)
-    y_step(2)
     piece(2, 0)
     piece(0, 3)
     piece(0, 1)
-    product(9)
+    reduce_y(4)
+    product(5, 0)
+    product(5, 1)
     x_far(3)
     x_far(1)
-    for dy in (3, 1):
-        piece(1, dy)
-        piece(3, dy)
+    product(6, 0)
+    product(6, 1)
+    piece(1, 3)
+    piece(3, 3)
+    piece(1, 1)
+    piece(3, 1)
     x_near(2)
+    reduce_y(5)
     piece(0, 2)
     piece(2, 3)
     piece(2, 1)
     x_far(2)
-    reduce_y(4)
+    reduce_y(6)
     piece(1, 2)
     piece(3, 2)
     piece(2, 2)
@@ -331,7 +353,7 @@
         return 0
 
     lax.fori_loop(0, 8, finish, 0)
-    for m in range(3):
+    for m in range(5):
         reduce_z(m)
 
     for cp in started:
@@ -347,7 +369,7 @@
     ]
     for cp in copies:
         cp.start()
-    gain_scaled = gain[...].astype(F32) * FACTOR
+    gain_scaled = gain[...].astype(F32).reshape(1, D) * FACTOR
 
     def grad_in(t, _):
         rows = pl.ds(pl.multiple_of(t * 64, 64), 64)
@@ -373,7 +395,7 @@
     anywhere = pl.BlockSpec(memory_space=pl.ANY)
     vmem = pl.BlockSpec(memory_space=pltpu.VMEM)
     dma = pltpu.SemaphoreType.DMA
-    gain_row = norm_gain.reshape(1, D)
+    gain_row = norm_gain
     act_v, back, prj, wgo, inv_v, mrow, pn, mn = pl.pallas_call(
         kernel,
         name="exchange",
@@ -409,10 +431,10 @@
             pltpu.VMEM((512, K), BF),
             pltpu.VMEM((512, K), BF),
             dma((3,)),
-            dma,
-            dma((10,)),
+            dma((2,)),
+            dma((7, 2)),
+            dma((7,)),
             dma((5,)),
-            dma((3,)),
             dma,
             dma((3,)),
             dma((3,)),
@@ -420,10 +442,10 @@
             dma((4, 2)),
             dma((4, 4, 2)),
             dma((4, 4)),
-            dma,
-            dma((10,)),
+            dma((2,)),
+            dma((7, 2)),
+            dma((7,)),
             dma((5,)),
-            dma((3,)),
             dma,
             dma((3,)),
             dma((3,)),

time: 95.2 us -> 93.6 us (0.983)
  local copies, waits for them, and re-layouts: 1.32 us -> 0.01 us
    reshape x1 -> x0, local copies, waits for them, and re-layouts: 1.31 us -> none  [shards(): gain_row = norm_gain.reshape(1, D)]
where the time goes in v3:
time: 93.6 us; the launch traced here: 93.2 us
  Pallas kernels  92.4 us (99%)
    pallas_call x1, Pallas kernels, shards(): pl.pallas_call(kernel, name='exchange', out_shape=(pltpu.VMEM((T, D), BF)...  89.6 us
    pallas_call x1, Pallas kernels, shards(): pl.pallas_call(finish_kernel, name='finish', out_shape=(jax.ShapeDtypeStr...  2.8 us

profile of v3, /device:TPU:1, one launch (start us, length us, event | category | flops | bytes accessed | tf_op | source)
XLA Modules:
  0.0 93.2 jit_solution(5260678217564113190)
XLA Ops:
  0.6 0.0 copy-start
  0.6 89.6 %exchange.1 = (bf16[512,4096]{1,0:T(8,128)(2,1)S(1)}, f32[32,512,128]{2,1,0:T(8,128)S(1)}, bf16[512,1024]{1,0:T(8,128)(2,1)S(1)}, bf16[512,1024]{1,0:T(8,128)(2,...) custom-call(s32[1,512,1024]{2,1,0:T(8,128)} %codes.1, ...), custom_call_target="tpu_custom_call" | custom-call | flops 12999999488 | bytes 14680064 | tf_op jit(solution)/shard_map/exchange/pallas_call | solution.py:399
  90.3 0.0 copy-done
  90.3 2.8 %finish.1 = (bf16[512,1024]{1,0:T(8,128)(2,1)}, bf16[512,4096]{1,0:T(8,128)(2,1)}, bf16[1,512,1024]{2,1,0:T(8,128)(2,1)}, f32[16,1024]{1,0:T(8,128)}, f32[16,1024]{1,0:T(8,128)}) custom-call(bf16[512,4096]{1,0:T(8,128)(2,1)S(1)} %get-tuple-element.13.act_v, f32[32,512,128]{2,1,0:T(8,128)S(1)} %get-tuple-element.14.back, ...), custom_call_target="tpu_custom_call" | custom-call | tf_op jit(solution)/shard_map/finish/pallas_call | solution.py:465
Async XLA Ops:
  0.6 89.6 %copy-start = (bf16[4096]{0:T(1024)(128)(2,1)S(1)}, bf16[4096]{0:T(1024)(128)(2,1)}, u32[]{:S(2)}) copy-start(bf16[4096]{0:T(1024)(128)(2,1)} %gain.3) | copy-start | bytes 24580

commit v4 on v3

--- a/solution.py
+++ b/solution.py
@@ -27,7 +27,7 @@
     codes, scales, params, moment, act, gain, cot,
     act_v, back, prj, wgo, inv_v, mrow, pn_o, mn_o,
     codes_v, cot_v, nrm, dec, g1r, g1s, g2r, g2s, g3r, wfull, acc,
-    rb, ra, ps, own, pr, zs, zr,
+    rb, ra, ps, own, pr, zs, zr, grow,
     lsem, bsem, asem, psem, zsem, gsem, g2sem, g3sem, zgsem, ygsem, xgsem, sbsem,
     bss, ass, pss, zss, gss, g2ss, g3ss, zgs, ygs, xgs, sbs,
 ):
@@ -121,6 +121,8 @@
 
     load_act.wait()
     gain_row = gain[...].astype(F32).reshape(1, D)
+    for j in range(32):
+        grow[j] = jnp.broadcast_to(gain_row[:, j * 128 : (j + 1) * 128] * FACTOR, (8, 128))
 
     def norm(t, _):
         rows = pl.ds(pl.multiple_of(t * 32, 32), 32)
@@ -284,8 +286,9 @@
         part = jnp.dot(lhs, w, preferred_element_type=F32)
         acc[...] = part if first else acc[...] + part
         b = lax.dot_general(cot_v[...], w, (((1,), (1,)), ((), ())), preferred_element_type=F32)
-        back[j] = b[:, :128]
-        back[j + 4] = b[:, 128:]
+        for i in range(2):
+            scaled = b[:, i * 128 : (i + 1) * 128] * grow[j + 4 * i][0:1, :]
+            back[j + 4 * i] = scaled * inv_v[...]
 
     arrived(rb.at[:, left], bsem.at[0])
     product(0, 0)
@@ -335,11 +338,14 @@
     piece(3, 1)
     x_near(2)
     reduce_y(5)
+    reduce_z(0)
+    reduce_z(1)
     piece(0, 2)
     piece(2, 3)
     piece(2, 1)
     x_far(2)
     reduce_y(6)
+    reduce_z(2)
     piece(1, 2)
     piece(3, 2)
     piece(2, 2)
@@ -353,14 +359,14 @@
         return 0
 
     lax.fori_loop(0, 8, finish, 0)
-    for m in range(5):
+    for m in (3, 4):
         reduce_z(m)
 
     for cp in started:
         cp.wait_send()
 
 
-def finish_kernel(act_v, back, prj, wgo, inv_v, mrow, gain, pn, mn, proj_o, ig_o, wg_o, pn_o, mn_o, grad, sem):
+def finish_kernel(act_v, back, prj, wgo, inv_v, mrow, pn, mn, proj_o, ig_o, wg_o, pn_o, mn_o, grad, sem):
     copies = [
         pltpu.make_async_copy(prj, proj_o, sem.at[8]),
         pltpu.make_async_copy(wgo, wg_o.at[0], sem.at[9]),
@@ -369,8 +375,6 @@
     ]
     for cp in copies:
         cp.start()
-    gain_scaled = gain[...].astype(F32).reshape(1, D) * FACTOR
-
     def grad_in(t, _):
         rows = pl.ds(pl.multiple_of(t * 64, 64), 64)
         inverse = inv_v[rows, :]
@@ -378,7 +382,7 @@
         for j in range(32):
             cols = slice(j * 128, (j + 1) * 128)
             a = act_v[rows, cols].astype(F32)
-            out = back[j, rows, :] * gain_scaled[:, cols] * inverse - a * m
+            out = back[j, rows, :] - a * m
             grad[rows, cols] = out.astype(BF)
         pltpu.make_async_copy(grad.at[rows], ig_o.at[rows], sem.at[t]).start()
         return 0
@@ -430,6 +434,7 @@
             pltpu.VMEM((1024, K), BF),
             pltpu.VMEM((512, K), BF),
             pltpu.VMEM((512, K), BF),
+            pltpu.VMEM((32, 8, 128), F32),
             dma((3,)),
             dma((2,)),
             dma((7, 2)),
@@ -472,11 +477,11 @@
             jax.ShapeDtypeStruct((16, K), F32),
             jax.ShapeDtypeStruct((16, K), F32),
         ),
-        in_specs=[vmem] * 9,
+        in_specs=[vmem] * 8,
         out_specs=(anywhere,) * 5,
         scratch_shapes=[pltpu.VMEM((T, D), BF), dma((12,))],
         compiler_params=pltpu.CompilerParams(vmem_limit_bytes=16 * 1024 * 1024),
-    )(act_v, back, prj, wgo, inv_v, mrow, gain_row, pn, mn)
+    )(act_v, back, prj, wgo, inv_v, mrow, pn, mn)
 
 
 def solution(mesh):

time: 93.6 us -> 93.6 us (level)
  no operation moved by 1% of the time
where the time goes in v4:
time: 93.6 us; the launch traced here: 93.1 us
  Pallas kernels  92.3 us (99%)
    pallas_call x1, Pallas kernels, shards(): pl.pallas_call(kernel, name='exchange', out_shape=(pltpu.VMEM((T, D), BF)...  89.5 us
    pallas_call x1, Pallas kernels, shards(): pl.pallas_call(finish_kernel, name='finish', out_shape=(jax.ShapeDtypeStr...  2.8 us

profile of v4, /device:TPU:1, one launch (start us, length us, event | category | flops | bytes accessed | tf_op | source)
XLA Modules:
  0.0 93.1 jit_solution(8170039879897320266)
XLA Ops:
  0.6 89.5 %exchange.1 = (bf16[512,4096]{1,0:T(8,128)(2,1)S(1)}, f32[32,512,128]{2,1,0:T(8,128)S(1)}, bf16[512,1024]{1,0:T(8,128)(2,1)S(1)}, bf16[512,1024]{1,0:T(8,128)(2,...) custom-call(s32[1,512,1024]{2,1,0:T(8,128)} %codes.1, ...), custom_call_target="tpu_custom_call" | custom-call | flops 12999999488 | bytes 14680064 | tf_op jit(solution)/shard_map/exchange/pallas_call | solution.py:403
  90.1 2.8 %finish.1 = (bf16[512,1024]{1,0:T(8,128)(2,1)}, bf16[512,4096]{1,0:T(8,128)(2,1)}, bf16[1,512,1024]{2,1,0:T(8,128)(2,1)}, f32[16,1024]{1,0:T(8,128)}, f32[16,1024]{1,0:T(8,128)}) custom-call(bf16[512,4096]{1,0:T(8,128)(2,1)S(1)} %get-tuple-element.13.act_v, f32[32,512,128]{2,1,0:T(8,128)S(1)} %get-tuple-element.14.back, ...), custom_call_target="tpu_custom_call" | custom-call | tf_op jit(solution)/shard_map/finish/pallas_call | solution.py:470
